TPU v7x, 128 devices: a whole 4x4x4 slice. The times are simulated.
128 devices in a mesh: dp: 8 (over z, core), fsdp: 16 (over x, y).
Axes of the slice: x: 4, y: 4, z: 4, core: 2. Of those that a mesh axis runs over, the one named last changes fastest.
Arguments:
- grads: bfloat16 [8, 224, 512, 512], P('dp', 'fsdp'), may hold values from -1 to 1
- owner: int32 [224], replicated, may hold values from 0 to 15, as said below
- roster: int32 [224], replicated, may hold values from 0 to 1, as said below
- left_stats: float32 [8, 16, 2, 512, 512], P('dp', 'fsdp'), may hold values from -1 to 20, as said below
- right_stats: float32 [8, 16, 2, 512, 512], P('dp', 'fsdp'), may hold values from -1 to 20, as said below
- left_root: bfloat16 [8, 16, 2, 512, 512], P('dp', 'fsdp'), may hold values from -1 to 6, as said below
- right_root: bfloat16 [8, 16, 2, 512, 512], P('dp', 'fsdp'), may hold values from -1 to 6, as said below
Outputs:
- updates: bfloat16 [224, 512, 512], P('fsdp', 'dp')
- new_left_stats: float32 [8, 16, 2, 512, 512], P('dp', 'fsdp')
- new_right_stats: float32 [8, 16, 2, 512, 512], P('dp', 'fsdp')
- new_left_root: bfloat16 [8, 16, 2, 512, 512], P('dp', 'fsdp')
- new_right_root: bfloat16 [8, 16, 2, 512, 512], P('dp', 'fsdp')
Inputs may be any that keep to these rules, and one draw needn't show every extreme that they name: `owner`: the 14 entries of one home (entries h * 14 to h * 14 + 13) name 14 different owners. `roster`: exactly 112 entries are 1. `left_stats`: every matrix is symmetric positive definite. `right_stats`: every matrix is symmetric positive definite. `left_root`: every matrix is symmetric positive definite. `right_root`: every matrix is symmetric positive definite.
All inputs are finite; a program needn't handle non-finite values. Where the computation divides by a largest or mean magnitude, that divisor is 1e-20 or more.
Results may differ from a plain program's by a relative error of at most 0.02.
Values may be sent and summed in bfloat16 or wider, within the bound.
A program may use at most 128 MiB of HBM per device.

v0:
```python
import jax
import jax.numpy as jnp
from jax import lax
from jax.experimental import pallas as pl
from jax.experimental.pallas import tpu as pltpu
from jax.sharding import PartitionSpec as P

BS = 512
HOMEB = 14
HALF = HOMEB // 2
NZ = 4
N_DP = 8
N_FSDP = 16
ROWS = BS // N_DP
R = 4
RR = ROWS // R
ROOT_STEPS = 6
decay_rate = 0.9
learn_rate = 10.0
BF = jnp.bfloat16
F32 = jnp.float32
MESH = pl.DeviceIdType.MESH


def dot(a, b, ca=1, cb=0):
    return lax.dot_general(a, b, (((ca,), (cb,)), ((), ())), preferred_element_type=F32)


def kernel(
    grads, owner, roster, left_stats, right_stats, left_root, right_root,
    updates, out_sl, out_sr, out_rl, out_rr,
    own, peer, b1p, b1m, b2p, b2m, fin, snd, rcv, grad,
    st, keep, mat, fac, cur, upd, turn, back, res, idx,
    own_sem, in_sem, core_s, core_r, z_s, z_r, pl_s, pl_r, dp_s, dp_r,
    h1_s, h1_r, h2_s, h2_r, out_sem,
):
    d = lax.axis_index("dp")
    h = lax.axis_index("fsdp")
    z = d // 2
    core = d % 2
    up = (z + 1) % NZ
    down = (z + 3) % NZ
    far = (z + 2) % NZ

    def at_dp(x):
        return {"dp": x, "fsdp": h}

    def at_fsdp(x):
        return {"dp": d, "fsdp": x}

    def own_copy(r):
        return pltpu.make_async_copy(grads.at[:, :, core, r], own.at[r], own_sem.at[r])

    def remote(src, dst, s, r, dev):
        return pltpu.make_async_remote_copy(
            src_ref=src, dst_ref=dst, send_sem=s, recv_sem=r, device_id=dev, device_id_type=MESH
        )

    def core_copy(r):
        return remote(grads.at[:, :, 1 - core, r], peer.at[r], core_s.at[r], core_r.at[r], at_dp(2 * z + 1 - core))

    dev_up = at_dp(2 * up + core)
    dev_down = at_dp(2 * down + core)
    lo = pl.ds(0, HALF)
    hi = pl.ds(HALF, HALF)

    def z_copy(kind, r):
        if kind == 0:
            src, dst, dev = own.at[r, lo, far], b1p.at[r], dev_up
        elif kind == 1:
            src, dst, dev = own.at[r, hi, far], b1m.at[r], dev_down
        elif kind == 2:
            src, dst, dev = own.at[r, hi, up], b2p.at[r, hi], dev_up
        elif kind == 3:
            src, dst, dev = own.at[r, lo, down], b2m.at[r, lo], dev_down
        elif kind == 4:
            src, dst, dev = own.at[r, lo, up], b2p.at[r, lo], dev_up
        else:
            src, dst, dev = own.at[r, hi, down], b2m.at[r, hi], dev_down
        return remote(src, dst, z_s.at[kind, r], z_r.at[kind, r], dev)

    def plane_send(r, o):
        return remote(snd.at[r, o], rcv.at[r, h], pl_s.at[r, o], pl_r.at[r, h], at_fsdp(o))

    def plane_recv(r, o):
        return remote(snd.at[r, o], rcv.at[r, o], pl_s.at[r, o], pl_r.at[r, o], at_fsdp(o))

    def rows_of(x, r):
        return pl.ds(pl.multiple_of(x * ROWS + r * RR, RR), RR)

    def dp_send(r, x):
        return remote(
            rcv.at[r, pl.ds(2 * x, 2)], grad.at[:, rows_of(d, r)], dp_s.at[r, x], dp_r.at[r, d], at_dp(x)
        )

    def dp_recv(r, x):
        return remote(
            rcv.at[r, pl.ds(2 * x, 2)], grad.at[:, rows_of(x, r)], dp_s.at[r, x], dp_r.at[r, x], at_dp(x)
        )

    def chunk(x):
        return pl.ds(pl.multiple_of(x * ROWS, ROWS), ROWS)

    def h1_send(j, x):
        return remote(upd.at[j, chunk(x)], turn.at[2 * d + j], h1_s.at[j, x], h1_r.at[2 * d + j], at_dp(x))

    def h1_recv(g, x):
        return remote(upd.at[0, chunk(x)], turn.at[g], h1_s.at[0, x], h1_r.at[g], at_dp(x))

    def h2_send(g):
        return remote(turn.at[g], back.at[h], h2_s.at[g], h2_r.at[h], at_fsdp(g))

    def h2_recv(o):
        return remote(turn.at[o], back.at[o], h2_s.at[o], h2_r.at[o], at_fsdp(o))

    def stat_in(i):
        return pltpu.make_async_copy((left_stats, right_stats)[i], st.at[i], in_sem.at[i])

    def keep_in(i):
        return pltpu.make_async_copy((left_root, right_root)[i], keep.at[i], in_sem.at[2 + i])

    def stat_out(i, j):
        return pltpu.make_async_copy(st.at[i, j], (out_sl, out_sr)[i].at[j], out_sem.at[i, j])

    def root_out(i, j):
        return pltpu.make_async_copy(keep.at[i, j], (out_rl, out_rr)[i].at[j], out_sem.at[2 + i, j])

    own_copy(0).start()
    for i in range(2):
        stat_in(i).start()
    for r in range(1, R):
        own_copy(r).start()
    for i in range(2):
        keep_in(i).start()

    barrier = pltpu.get_barrier_semaphore()

    @pl.loop(1, N_DP)
    def _(i):
        pl.semaphore_signal(barrier, inc=1, device_id=at_dp((d + i) % N_DP), device_id_type=MESH)

    @pl.loop(1, N_FSDP)
    def _(i):
        pl.semaphore_signal(barrier, inc=1, device_id=at_fsdp((h + i) % N_FSDP), device_id_type=MESH)

    pl.semaphore_wait(barrier, N_DP + N_FSDP - 2)

    @pl.loop(0, R)
    def _(r):
        core_copy(r).start()

    @pl.loop(0, N_FSDP)
    def _(o):
        place = jnp.int32(HOMEB)
        for k in range(HOMEB):
            place = jnp.where(owner[h * HOMEB + k] == o, jnp.int32(k), place)
        idx[o] = place

    fin[HOMEB] = jnp.zeros((RR, BS), BF)
    for i in range(2):
        stat_in(i).wait()
    for i in range(2):
        keep_in(i).wait()

    ii = lax.broadcasted_iota(jnp.int32, (BS, BS), 0)
    jj = lax.broadcasted_iota(jnp.int32, (BS, BS), 1)

    def factor(m):
        return (jnp.where(ii == jj, 1.25, 0.0) - 0.25 * m).astype(BF)

    def root_step(t):
        slot = t // 3
        sweep = t % 3

        @pl.when(sweep == 0)
        def _():
            for i in range(2):
                a = st[i, slot]
                bound = jnp.max(jnp.sum(jnp.abs(a), axis=0, keepdims=True), axis=1, keepdims=True)
                m = a * (1.0 / bound)
                f = factor(m)
                mat[i] = m.astype(BF)
                fac[i] = f
                first = lax.rsqrt(jnp.sqrt(bound)).astype(BF).astype(F32)
                cur[i] = (first * f.astype(F32)).astype(BF)

        for i in range(2):
            f = fac[i]
            f2 = dot(f, f).astype(BF)
            f4 = dot(f2, f2).astype(BF)
            m = dot(f4, mat[i])
            mat[i] = m.astype(BF)
            f = factor(m)
            fac[i] = f
            cur[i] = dot(cur[i], f).astype(BF)

        @pl.when(sweep == 2)
        def _():
            flag = jnp.int32(0)
            for k in range(HOMEB):
                spot = (2 * d + slot) * HOMEB + k
                flag += jnp.where(owner[spot] == h, roster[spot], 0)
            for i in range(2):
                keep[i, slot] = jnp.where(flag > 0, cur[i], keep[i, slot])

    def stage_a(r):
        own_copy(r).wait()
        core_copy(r).wait_recv()

        @pl.loop(0, HOMEB)
        def _(k):
            own[r, k] = (own[r, k].astype(F32) + peer[r, k].astype(F32)).astype(BF)

        for kind in range(4):
            z_copy(kind, r).start()

    def stage_b(r):
        z_copy(0, r).wait_recv()
        own[r, lo, up] = (own[r, lo, up].astype(F32) + b1p[r].astype(F32)).astype(BF)
        z_copy(4, r).start()
        z_copy(1, r).wait_recv()
        own[r, hi, down] = (own[r, hi, down].astype(F32) + b1m[r].astype(F32)).astype(BF)
        z_copy(5, r).start()

    def stage_c(r):
        for kind in range(2, 6):
            z_copy(kind, r).wait_recv()

        fin[pl.ds(0, HOMEB)] = (
            own[r, :, z].astype(F32) + b2p[r].astype(F32) + b2m[r].astype(F32)
        ).astype(BF)

        @pl.loop(0, N_FSDP)
        def _(o):
            snd[r, o] = fin[idx[o]]

        rcv[r, h] = snd[r, h]

        @pl.loop(1, N_FSDP)
        def _(i):
            plane_send(r, (h + i) % N_FSDP).start()

    def stage_d(r):
        @pl.loop(1, N_FSDP)
        def _(i):
            plane_recv(r, (h + i) % N_FSDP).wait_recv()

        grad[:, rows_of(d, r)] = rcv[r, pl.ds(2 * d, 2)]

        @pl.loop(1, N_DP)
        def _(i):
            dp_send(r, (d + i) % N_DP).start()

    @pl.loop(0, R + 3)
    def _(t):
        @pl.when(t < R)
        def _():
            stage_a(t)

        @pl.when(jnp.logical_and(t >= 1, t < R + 1))
        def _():
            stage_b(t - 1)

        @pl.when(jnp.logical_and(t >= 2, t < R + 2))
        def _():
            stage_c(t - 2)

        @pl.when(t >= 3)
        def _():
            stage_d(t - 3)

        @pl.when(t < ROOT_STEPS)
        def _():
            root_step(t)

    for i in range(2):
        for j in range(2):
            root_out(i, j).start()

    @pl.loop(0, R)
    def _(r):
        @pl.loop(1, N_DP)
        def _(i):
            dp_recv(r, (d + i) % N_DP).wait_recv()

    @pl.loop(0, 2)
    def _(j):
        g = grad[j]
        half = dot(keep[0, j], g).astype(BF)
        direction = dot(half, keep[1, j])
        g = g.astype(F32)
        count = float(BS * BS)
        grad_sq = jnp.sum(jnp.sum(g * g, axis=0, keepdims=True), axis=1, keepdims=True)
        dir_sq = jnp.sum(jnp.sum(direction * direction, axis=0, keepdims=True), axis=1, keepdims=True)
        ratio = jnp.sqrt(grad_sq / count) / jnp.sqrt(dir_sq / count + 1e-06)
        upd[j] = (-learn_rate * direction * ratio).astype(BF)
        turn[2 * d + j] = upd[j, chunk(d)]

        @pl.loop(1, N_DP)
        def _(i):
            h1_send(j, (d + i) % N_DP).start()

    def forward(i, j):
        x = (d + i) % N_DP
        g = 2 * x + j

        @pl.when(i > 0)
        def _():
            h1_recv(g, x).wait_recv()

        @pl.when(g != h)
        def _():
            h2_send(g).start()

        @pl.when(g == h)
        def _():
            back[h] = turn[h]

    @pl.loop(0, 2)
    def _(j):
        @pl.loop(0, N_DP)
        def _(i):
            forward(i, j)

    @pl.loop(0, 2)
    def _(j):
        g = grad[j]
        st[0, j] = decay_rate * st[0, j] + (1.0 - decay_rate) * dot(g, g, 1, 1)
        st[1, j] = decay_rate * st[1, j] + (1.0 - decay_rate) * dot(g, g, 0, 0)

    for i in range(2):
        for j in range(2):
            stat_out(i, j).start()

    @pl.loop(1, N_FSDP)
    def _(i):
        h2_recv((h + i) % N_FSDP).wait_recv()

    @pl.loop(0, HOMEB)
    def _(k):
        res[k] = back[owner[h * HOMEB + k]]

    last = pltpu.make_async_copy(res, updates, out_sem.at[4, 0])
    last.start()

    @pl.loop(0, R)
    def _(r):
        core_copy(r).wait_send()
        for kind in range(6):
            z_copy(kind, r).wait_send()

        @pl.loop(1, N_FSDP)
        def _(i):
            plane_send(r, (h + i) % N_FSDP).wait_send()

        @pl.loop(1, N_DP)
        def _(i):
            dp_send(r, (d + i) % N_DP).wait_send()

    @pl.loop(1, N_DP)
    def _(i):
        for j in range(2):
            h1_send(j, (d + i) % N_DP).wait_send()

    @pl.loop(1, N_FSDP)
    def _(i):
        h2_send((h + i) % N_FSDP).wait_send()

    for i in range(2):
        for j in range(2):
            root_out(i, j).wait()
            stat_out(i, j).wait()
    last.wait()


def local(grads, owner, roster, left_stats, right_stats, left_root, right_root):
    anywhere = pl.BlockSpec(memory_space=pl.ANY)
    scalars = pl.BlockSpec(memory_space=pltpu.SMEM)
    dma = pltpu.SemaphoreType.DMA
    shape = jax.ShapeDtypeStruct
    outs = pl.pallas_call(
        kernel,
        out_shape=(
            shape((HOMEB, ROWS, BS), BF),
            shape((2, BS, BS), F32),
            shape((2, BS, BS), F32),
            shape((2, BS, BS), BF),
            shape((2, BS, BS), BF),
        ),
        in_specs=[anywhere, scalars, scalars] + [anywhere] * 4,
        out_specs=[anywhere] * 5,
        scratch_shapes=[
            pltpu.VMEM((R, HOMEB, NZ, RR, BS), BF),
            pltpu.VMEM((R, HOMEB, NZ, RR, BS), BF),
            pltpu.VMEM((R, HALF, RR, BS), BF),
            pltpu.VMEM((R, HALF, RR, BS), BF),
            pltpu.VMEM((R, HOMEB, RR, BS), BF),
            pltpu.VMEM((R, HOMEB, RR, BS), BF),
            pltpu.VMEM((HOMEB + 1, RR, BS), BF),
            pltpu.VMEM((R, N_FSDP, RR, BS), BF),
            pltpu.VMEM((R, N_FSDP, RR, BS), BF),
            pltpu.VMEM((2, BS, BS), BF),
            pltpu.VMEM((2, 2, BS, BS), F32),
            pltpu.VMEM((2, 2, BS, BS), BF),
            pltpu.VMEM((2, BS, BS), BF),
            pltpu.VMEM((2, BS, BS), BF),
            pltpu.VMEM((2, BS, BS), BF),
            pltpu.VMEM((2, BS, BS), BF),
            pltpu.VMEM((N_FSDP, ROWS, BS), BF),
            pltpu.VMEM((N_FSDP, ROWS, BS), BF),
            pltpu.VMEM((HOMEB, ROWS, BS), BF),
            pltpu.SMEM((N_FSDP,), jnp.int32),
            dma((R,)),
            dma((4,)),
            dma((R,)),
            dma((R,)),
            dma((6, R)),
            dma((6, R)),
            dma((R, N_FSDP)),
            dma((R, N_FSDP)),
            dma((R, N_DP)),
            dma((R, N_DP)),
            dma((2, N_DP)),
            dma((N_FSDP,)),
            dma((N_FSDP,)),
            dma((N_FSDP,)),
            dma((5, 2)),
        ],
        compiler_params=pltpu.CompilerParams(
            collective_id=0, has_side_effects=True, vmem_limit_bytes=56 * 1024 * 1024
        ),
        cost_estimate=pl.CostEstimate(flops=16 * 10**9, bytes_accessed=24 * 10**6, transcendentals=0),
        name="shampoo",
    )(
        grads.reshape(HOMEB, NZ, 2, R, RR, BS),
        owner,
        roster,
        left_stats[0, 0],
        right_stats[0, 0],
        left_root[0, 0],
        right_root[0, 0],
    )
    result, new_left, new_right, roots_left, roots_right = outs
    return (result, new_left[None, None], new_right[None, None], roots_left[None, None], roots_right[None, None])


def solution(mesh):
    placed = P("dp", "fsdp", None, None, None)
    return jax.shard_map(
        local,
        mesh=mesh,
        in_specs=(P("dp", "fsdp", None, None), P(), P(), placed, placed, placed, placed),
        out_specs=(P("fsdp", "dp", None), placed, placed, placed, placed),
        check_vma=False,
    )
```

profile of v0, /device:TPU:15, one launch (start us, length us, event | category | flops | bytes accessed | tf_op | source)
XLA Modules:
  0.0 99.8 jit_solution(10373618335798632124)
XLA Ops:
  0.6 89.2 %shampoo.1 = (bf16[14,64,512]{2,1,0:T(8,128)(2,1)}, f32[2,512,512]{2,1,0:T(8,128)}, f32[2,512,512]{2,1,0:T(8,128)}, bf16[2,512,512]{2,1,0:T(8,128)(2,1)}, bf16[2,512,512]{2,1,0:T(8,128)(2,1)}) custom-call(bf16[14,4,2,4,16,512]{5,4,3,2,1,0:T(8,128)(2,1)} %bitcast.13, s32[224]{0:T(256)} %owner.1, s32[224]{0:T(256)} %roster.1, f32[2,512,512]{2,1,0:T(8,128)} %bitcast.14, ...), custom_call_target="tpu_custom_call" | custom-call | flops 16000000000 | bytes 24000000 | tf_op jit(solution)/shard_map/shampoo/pallas_call | solution.py:381
  89.9 2.2 %copy.17 = bf16[14,64,512]{2,1,0:T(8,128)(2,1)} copy(bf16[14,64,512]{2,1,0:T(8,128)(2,1)} %get-tuple-element.20) | data formatting | bytes 1835008
  92.0 0.0 copy-start
  92.0 3.2 %copy.18 = f32[1,1,2,512,512]{4,3,2,1,0:T(8,128)} copy(f32[1,1,2,512,512]{4,3,2,1,0:T(8,128)} %bitcast.10) | data formatting | bytes 4194304
  95.3 0.0 copy-done
  95.3 0.0 copy-start.2
  95.3 1.3 %copy.19 = f32[1,1,2,512,512]{4,3,2,1,0:T(8,128)} copy(f32[1,1,2,512,512]{4,3,2,1,0:T(8,128)S(1)} %bitcast.9) | data formatting | bytes 4194304
  96.6 0.6 copy-done.2
  97.2 0.0 copy-start.1
  97.2 1.0 copy.20
  98.2 0.6 copy-done.1
  98.8 1.0 copy.21
Async XLA Ops:
  92.0 3.2 %copy-start = (f32[2,512,512]{2,1,0:T(8,128)S(1)}, f32[2,512,512]{2,1,0:T(8,128)}, u32[]{:S(2)}) copy-start(f32[2,512,512]{2,1,0:T(8,128)} %get-tuple-element.12) | copy-start | bytes 6291460
  95.3 2.0 %copy-start.2 = (bf16[2,512,512]{2,1,0:T(8,128)(2,1)S(1)}, bf16[2,512,512]{2,1,0:T(8,128)(2,1)}, u32[]{:S(2)}) copy-start(bf16[2,512,512]{2,1,0:T(8,128)(2,1)} %get-tuple-element.13) | copy-start | bytes 3145732
  97.2 1.6 %copy-start.1 = (bf16[2,512,512]{2,1,0:T(8,128)(2,1)S(1)}, bf16[2,512,512]{2,1,0:T(8,128)(2,1)}, u32[]{:S(2)}) copy-start(bf16[2,512,512]{2,1,0:T(8,128)(2,1)} %get-tuple-element.14) | copy-start | bytes 3145732
where the time goes:
time: 100 us; the launch traced here: 99.8 us
  Pallas kernels  89.2 us (89%)
  local copies, waits for them, and re-layouts  9.93 us (10%)
    pallas_call x1, Pallas kernels, local(): pl.pallas_call(kernel, out_shape=(shape((HOMEB, ROWS, BS), BF), shape((2,...  89.2 us
    unnamed x11, local copies, waits for them, and re-layouts  9.93 us

commit v1 on v0

v1 whole, which is shorter than its diff:
```python
import functools

import jax
import jax.numpy as jnp
from jax import lax
from jax.experimental import pallas as pl
from jax.experimental.pallas import tpu as pltpu
from jax.sharding import PartitionSpec as P

BS = 512
HOMEB = 14
HALF = HOMEB // 2
NZ = 4
N_DP = 8
N_FSDP = 16
ROWS = BS // N_DP
R = 4
RR = ROWS // R
LAST = R - 1
ROOT_STEPS = 6
STEPS = 9
PIECES = 2
PIECE = ROWS // PIECES
decay_rate = 0.9
learn_rate = 10.0
BF = jnp.bfloat16
F32 = jnp.float32
MESH = pl.DeviceIdType.MESH


def dot(a, b, ca=1, cb=0):
    return lax.dot_general(a, b, (((ca,), (cb,)), ((), ())), preferred_element_type=F32)


def kernel(
    grads, owner_in, roster_in, left_stats, right_stats, left_root, right_root,
    res, st, keep,
    own, peer, mix, b1p, b1m, b2p, b2m, fin, snd, rcv, grad,
    mat, fac, cur, upd, turn, back, idx, owner, roster,
    own_sem, in_sem, core_s, core_r, x_s, x_r, z_s, z_r, pl_s, pl_r, dp_s, dp_r, ex_s, ex_r,
    h1_s, h1_r, h2_s, h2_r,
):
    d = lax.axis_index("dp")
    h = lax.axis_index("fsdp")
    z = d // 2
    core = d % 2
    x = h // 4
    y = h % 4
    up = (z + 1) % NZ
    down = (z + 3) % NZ
    far = (z + 2) % NZ

    def at_dp(x):
        return {"dp": x, "fsdp": h}

    def at_fsdp(x):
        return {"dp": d, "fsdp": x}

    def own_copy(r):
        return pltpu.make_async_copy(grads.at[:, :, core, r], own.at[r], own_sem.at[r])

    def remote(src, dst, s, r, dev):
        return pltpu.make_async_remote_copy(
            src_ref=src, dst_ref=dst, send_sem=s, recv_sem=r, device_id=dev, device_id_type=MESH
        )

    def core_copy(r):
        return remote(grads.at[:, :, 1 - core, r], peer.at[r], core_s.at[r], core_r.at[r], at_dp(2 * z + 1 - core))

    dev_up = at_dp(2 * up + core)
    dev_down = at_dp(2 * down + core)
    lo = pl.ds(0, HALF)
    hi = pl.ds(HALF, HALF)

    def held(r, mixed):
        return mix if mixed else own.at[r]

    def z_copy(kind, r, mixed):
        part = held(r, mixed)
        if kind == 0:
            src, dst, dev = part.at[lo, far], b1p.at[r], dev_up
        elif kind == 1:
            src, dst, dev = part.at[hi, far], b1m.at[r], dev_down
        elif kind == 2:
            src, dst, dev = part.at[hi, up], b2p.at[r, hi], dev_up
        elif kind == 3:
            src, dst, dev = part.at[lo, down], b2m.at[r, lo], dev_down
        elif kind == 4:
            src, dst, dev = part.at[lo, up], b2p.at[r, lo], dev_up
        else:
            src, dst, dev = part.at[hi, down], b2m.at[r, hi], dev_down
        return remote(src, dst, z_s.at[kind, r], z_r.at[kind, r], dev)

    def x_send(i):
        q = (x + i) % 4
        return remote(own.at[LAST, :, q], mix.at[:, x], x_s.at[q], x_r.at[x], at_fsdp(4 * q + y))

    def x_recv(i):
        q = (x + i) % 4
        return remote(own.at[LAST, :, q], mix.at[:, q], x_s.at[q], x_r.at[q], at_fsdp(4 * q + y))

    def plane_send(r, o):
        return remote(snd.at[r, o], rcv.at[r, h], pl_s.at[r, o], pl_r.at[r, h], at_fsdp(o))

    def plane_recv(r, o):
        return remote(snd.at[r, o], rcv.at[r, o], pl_s.at[r, o], pl_r.at[r, o], at_fsdp(o))

    def rows_of(x, r):
        return pl.ds(pl.multiple_of(x * ROWS + r * RR, RR), RR)

    def dp_send(r, x):
        return remote(
            rcv.at[r, pl.ds(2 * x, 2)], grad.at[:, rows_of(d, r)], dp_s.at[r, x], dp_r.at[r, d], at_dp(x)
        )

    def dp_recv(r, x):
        return remote(
            rcv.at[r, pl.ds(2 * x, 2)], grad.at[:, rows_of(x, r)], dp_s.at[r, x], dp_r.at[r, x], at_dp(x)
        )

    def ex_send(o):
        return remote(
            snd.at[LAST, o], grad.at[y % 2, rows_of(2 * x + core, LAST)],
            ex_s.at[o], ex_r.at[(y % 2) * N_DP + 2 * x + core],
            {"dp": 2 * z + y // 2, "fsdp": o},
        )

    def ex_recv(i):
        return remote(
            snd.at[LAST, 0], grad.at[i // N_DP, rows_of(i % N_DP, LAST)], ex_s.at[0], ex_r.at[i],
            {"dp": d, "fsdp": (h + 1) % N_FSDP},
        )

    def chunk(x):
        return pl.ds(pl.multiple_of(x * ROWS, ROWS), ROWS)

    def piece(x, p):
        return pl.ds(pl.multiple_of(x * ROWS + p * PIECE, PIECE), PIECE)

    def h1_send(j, p, x):
        return remote(
            upd.at[j, piece(x, p)], turn.at[2 * d + j, p], h1_s.at[j, p, x], h1_r.at[2 * d + j, p], at_dp(x)
        )

    def h1_recv(g, p, x):
        return remote(upd.at[0, piece(x, p)], turn.at[g, p], h1_s.at[0, p, x], h1_r.at[g, p], at_dp(x))

    def h2_send(g, p):
        return remote(turn.at[g, p], back.at[h, p], h2_s.at[g, p], h2_r.at[h, p], at_fsdp(g))

    def h2_recv(o, p):
        return remote(turn.at[o, p], back.at[o, p], h2_s.at[o, p], h2_r.at[o, p], at_fsdp(o))

    def stat_in(i):
        return pltpu.make_async_copy((left_stats, right_stats)[i], st.at[i], in_sem.at[i])

    def keep_in(i):
        return pltpu.make_async_copy((left_root, right_root)[i], keep.at[i], in_sem.at[2 + i])

    tables = [
        pltpu.make_async_copy(owner_in, owner, in_sem.at[4]),
        pltpu.make_async_copy(roster_in, roster, in_sem.at[5]),
    ]
    for table in tables:
        table.start()

    @pl.loop(0, R)
    def _(r):
        own_copy(r).start()

    barrier = pltpu.get_barrier_semaphore()

    @pl.loop(1, N_DP)
    def _(i):
        pl.semaphore_signal(barrier, inc=1, device_id=at_dp((d + i) % N_DP), device_id_type=MESH)

    @pl.loop(1, N_FSDP)
    def _(i):
        pl.semaphore_signal(barrier, inc=1, device_id=at_fsdp((h + i) % N_FSDP), device_id_type=MESH)

    @pl.loop(0, N_DP)
    def _(i):
        there = {"dp": 2 * z + 1 - core, "fsdp": (i // 2) * 4 + 2 * core + i % 2}
        pl.semaphore_signal(barrier, inc=1, device_id=there, device_id_type=MESH)

    pl.semaphore_wait(barrier, N_DP + N_FSDP - 2 + jnp.where(y // 2 == core, 0, N_FSDP))

    core_copy(0).start()
    core_copy(LAST).start()

    def begin():
        for i in range(2):
            stat_in(i).start()
        for i in range(2):
            keep_in(i).start()

        for table in tables:
            table.wait()

        @pl.loop(0, N_FSDP)
        def _(o):
            for i, home in enumerate((h, 4 * z + y)):
                place = jnp.int32(HOMEB)
                for k in range(HOMEB):
                    place = jnp.where(owner[home * HOMEB + k] == o, jnp.int32(k), place)
                idx[i, o] = place

        fin[HOMEB] = jnp.zeros((RR, BS), BF)
        for i in range(2):
            stat_in(i).wait()
        for i in range(2):
            keep_in(i).wait()

    ii = lax.broadcasted_iota(jnp.int32, (BS, BS), 0)
    jj = lax.broadcasted_iota(jnp.int32, (BS, BS), 1)

    def factor(m):
        return (jnp.where(ii == jj, 1.25, 0.0) - 0.25 * m).astype(BF)

    def root_step(t):
        slot = t // 3
        sweep = t % 3

        @pl.when(sweep == 0)
        def _():
            for i in range(2):
                a = st[i, slot]
                bound = jnp.max(jnp.sum(jnp.abs(a), axis=0, keepdims=True), axis=1, keepdims=True)
                m = a * (1.0 / bound)
                f = factor(m)
                mat[i] = m.astype(BF)
                fac[i] = f
                first = lax.rsqrt(jnp.sqrt(bound)).astype(BF).astype(F32)
                cur[i] = (first * f.astype(F32)).astype(BF)

        for i in range(2):
            f = fac[i]
            f2 = dot(f, f).astype(BF)
            f4 = dot(f2, f2).astype(BF)
            m = dot(f4, mat[i])
            mat[i] = m.astype(BF)
            f = factor(m)
            fac[i] = f
            cur[i] = dot(cur[i], f).astype(BF)

        @pl.when(sweep == 2)
        def _():
            flag = jnp.int32(0)
            for k in range(HOMEB):
                spot = (2 * d + slot) * HOMEB + k
                flag += jnp.where(owner[spot] == h, roster[spot], 0)
            for i in range(2):
                keep[i, slot] = jnp.where(flag > 0, cur[i], keep[i, slot])

    def stage_a(r):
        own_copy(r).wait()
        core_copy(r).wait_recv()

        @pl.when(r == 0)
        def _():
            core_copy(1).start()

        @pl.when(r == LAST)
        def _():
            core_copy(2).start()

        @pl.loop(0, HOMEB)
        def _(k):
            own[r, k] = own[r, k] + peer[r, k]

    def begin_z(r, mixed):
        for kind in range(2):
            z_copy(kind, r, mixed).start()

        @pl.when(r != LAST)
        def _():
            for kind in range(2, 4):
                z_copy(kind, r, mixed).start()

    def begin_x():
        for i in (2, 1, 3):
            x_send(i).start()
        mix[:, x] = own[LAST, :, x]

    def end_x():
        for i in (2, 1, 3):
            x_recv(i).wait_recv()
        begin_z(LAST, True)

    def stage_b(r, mixed):
        part = held(r, mixed)
        z_copy(0, r, mixed).wait_recv()
        part[lo, up] = part[lo, up] + b1p[r]
        z_copy(4, r, mixed).start()
        z_copy(1, r, mixed).wait_recv()
        part[hi, down] = part[hi, down] + b1m[r]
        z_copy(5, r, mixed).start()

        @pl.when(r == LAST)
        def _():
            for kind in range(2, 4):
                z_copy(kind, r, mixed).start()

    def stage_c(r, mixed):
        part = held(r, mixed)
        for kind in range(2, 6):
            z_copy(kind, r, mixed).wait_recv()

        fin[pl.ds(0, HOMEB)] = (
            part[:, z].astype(F32) + b2p[r].astype(F32) + b2m[r].astype(F32)
        ).astype(BF)

        @pl.loop(0, N_FSDP)
        def _(o):
            snd[r, o] = fin[idx[1 if mixed else 0, o]]

        if mixed:
            @pl.loop(1, N_FSDP)
            def _(i):
                ex_send((h + 5 * i) % N_FSDP).start()

            @pl.when(y // 2 != core)
            def _():
                ex_send(h).start()

            @pl.when(y // 2 == core)
            def _():
                grad[y % 2, rows_of(2 * x + core, r)] = snd[r, h]
        else:
            rcv[r, h] = snd[r, h]

            @pl.loop(1, N_FSDP)
            def _(i):
                plane_send(r, (h + 5 * i) % N_FSDP).start()

    def stage_d(r):
        @pl.loop(1, N_FSDP)
        def _(i):
            plane_recv(r, (h + i) % N_FSDP).wait_recv()

        grad[:, rows_of(d, r)] = rcv[r, pl.ds(2 * d, 2)]

        @pl.loop(1, N_DP)
        def _(i):
            dp_send(r, (d + 3 * i) % N_DP).start()

    def either(t, *steps):
        return functools.reduce(jnp.logical_or, [t == step for step in steps])

    @pl.loop(0, STEPS)
    def _(t):
        @pl.when(t < R)
        def _():
            stage_a(jnp.where(t == 1, LAST, jnp.maximum(t - 1, 0)))

        @pl.when(either(t, 0, 2, 3))
        def _():
            begin_z(jnp.maximum(t - 1, 0), False)

        @pl.when(t == 1)
        def _():
            begin_x()

        @pl.when(t == 2)
        def _():
            begin()

        @pl.when(either(t, 2, 3, 4))
        def _():
            stage_b(t - 2, False)

        @pl.when(t == 5)
        def _():
            end_x()

        @pl.when(t == 6)
        def _():
            stage_b(LAST, True)

        @pl.when(either(t, 4, 5, 6))
        def _():
            stage_c(t - 4, False)

        @pl.when(either(t, 5, 6, 7))
        def _():
            stage_d(t - 5)

        @pl.when(t == 8)
        def _():
            stage_c(LAST, True)

        @pl.when(jnp.logical_and(t >= 2, t < 2 + ROOT_STEPS))
        def _():
            root_step(t - 2)

    def from_me(i):
        return jnp.logical_and(i == (y % 2) * N_DP + 2 * x + core, y // 2 == core)

    @pl.loop(0, LAST)
    def _(r):
        @pl.loop(1, N_DP)
        def _(i):
            dp_recv(r, (d + i) % N_DP).wait_recv()

    @pl.loop(0, 2 * N_DP)
    def _(i):
        @pl.when(jnp.logical_not(from_me(i)))
        def _():
            ex_recv(i).wait_recv()

    @pl.loop(0, 2)
    def _(j):
        g = grad[j]
        half = dot(keep[0, j], g).astype(BF)
        direction = dot(half, keep[1, j])
        g = g.astype(F32)
        count = float(BS * BS)
        grad_sq = jnp.sum(jnp.sum(g * g, axis=0, keepdims=True), axis=1, keepdims=True)
        dir_sq = jnp.sum(jnp.sum(direction * direction, axis=0, keepdims=True), axis=1, keepdims=True)
        ratio = jnp.sqrt(grad_sq / count) / jnp.sqrt(dir_sq / count + 1e-06)
        upd[j] = (-learn_rate * direction * ratio).astype(BF)
        for p in range(PIECES):
            turn[2 * d + j, p] = upd[j, piece(d, p)]

            @pl.loop(1, N_DP)
            def _(i):
                h1_send(j, p, (d + 3 * i) % N_DP).start()

    def forward(i, j, p):
        x = (d + 5 * i) % N_DP
        g = 2 * x + j

        @pl.when(i > 0)
        def _():
            h1_recv(g, p, x).wait_recv()

        @pl.when(g != h)
        def _():
            h2_send(g, p).start()

        @pl.when(g == h)
        def _():
            back[h, p] = turn[h, p]

    @pl.loop(0, 2)
    def _(j):
        @pl.loop(0, PIECES)
        def _(p):
            @pl.loop(0, N_DP)
            def _(i):
                forward(i, j, p)

    @pl.loop(0, 2)
    def _(j):
        g = grad[j]
        st[0, j] = decay_rate * st[0, j] + (1.0 - decay_rate) * dot(g, g, 1, 1)
        st[1, j] = decay_rate * st[1, j] + (1.0 - decay_rate) * dot(g, g, 0, 0)

    @pl.loop(1, N_FSDP)
    def _(i):
        for p in range(PIECES):
            h2_recv((h + i) % N_FSDP, p).wait_recv()

    @pl.loop(0, HOMEB)
    def _(k):
        for p in range(PIECES):
            res[k, pl.ds(p * PIECE, PIECE)] = back[owner[h * HOMEB + k], p]

    @pl.loop(0, R)
    def _(r):
        core_copy(r).wait_send()
        for kind in range(6):
            z_copy(kind, r, False).wait_send()

    for i in (1, 2, 3):
        x_send(i).wait_send()

    @pl.loop(0, LAST)
    def _(r):
        @pl.loop(1, N_FSDP)
        def _(i):
            plane_send(r, (h + i) % N_FSDP).wait_send()

        @pl.loop(1, N_DP)
        def _(i):
            dp_send(r, (d + i) % N_DP).wait_send()

    @pl.loop(1, N_FSDP)
    def _(i):
        ex_send((h + i) % N_FSDP).wait_send()

    @pl.when(y // 2 != core)
    def _():
        ex_send(h).wait_send()

    @pl.loop(0, PIECES)
    def _(p):
        @pl.loop(1, N_DP)
        def _(i):
            for j in range(2):
                h1_send(j, p, (d + i) % N_DP).wait_send()

        @pl.loop(1, N_FSDP)
        def _(i):
            h2_send((h + i) % N_FSDP, p).wait_send()


def finish(res, st, keep, updates, out_sl, out_sr, out_rl, out_rr, sem):
    copies = [pltpu.make_async_copy(res, updates, sem.at[8])]
    for i in range(2):
        for j in range(2):
            copies.append(pltpu.make_async_copy(st.at[i, j], (out_sl, out_sr)[i].at[j], sem.at[2 * i + j]))
            copies.append(pltpu.make_async_copy(keep.at[i, j], (out_rl, out_rr)[i].at[j], sem.at[4 + 2 * i + j]))
    for copy in copies:
        copy.start()
    for copy in copies:
        copy.wait()


def local(grads, owner, roster, left_stats, right_stats, left_root, right_root):
    anywhere = pl.BlockSpec(memory_space=pl.ANY)
    dma = pltpu.SemaphoreType.DMA
    shape = jax.ShapeDtypeStruct
    outs = pl.pallas_call(
        kernel,
        out_shape=(
            pltpu.VMEM((HOMEB, ROWS, BS), BF),
            pltpu.VMEM((2, 2, BS, BS), F32),
            pltpu.VMEM((2, 2, BS, BS), BF),
        ),
        in_specs=[anywhere] * 7,
        out_specs=[pl.BlockSpec(memory_space=pltpu.VMEM)] * 3,
        scratch_shapes=[
            pltpu.VMEM((R, HOMEB, NZ, RR, BS), BF),
            pltpu.VMEM((R, HOMEB, NZ, RR, BS), BF),
            pltpu.VMEM((HOMEB, NZ, RR, BS), BF),
            pltpu.VMEM((R, HALF, RR, BS), BF),
            pltpu.VMEM((R, HALF, RR, BS), BF),
            pltpu.VMEM((R, HOMEB, RR, BS), BF),
            pltpu.VMEM((R, HOMEB, RR, BS), BF),
            pltpu.VMEM((HOMEB + 1, RR, BS), BF),
            pltpu.VMEM((R, N_FSDP, RR, BS), BF),
            pltpu.VMEM((R, N_FSDP, RR, BS), BF),
            pltpu.VMEM((2, BS, BS), BF),
            pltpu.VMEM((2, BS, BS), BF),
            pltpu.VMEM((2, BS, BS), BF),
            pltpu.VMEM((2, BS, BS), BF),
            pltpu.VMEM((2, BS, BS), BF),
            pltpu.VMEM((N_FSDP, PIECES, PIECE, BS), BF),
            pltpu.VMEM((N_FSDP, PIECES, PIECE, BS), BF),
            pltpu.SMEM((2, N_FSDP), jnp.int32),
            pltpu.SMEM((N_FSDP * HOMEB,), jnp.int32),
            pltpu.SMEM((N_FSDP * HOMEB,), jnp.int32),
            dma((R,)),
            dma((6,)),
            dma((R,)),
            dma((R,)),
            dma((4,)),
            dma((4,)),
            dma((6, R)),
            dma((6, R)),
            dma((R, N_FSDP)),
            dma((R, N_FSDP)),
            dma((R, N_DP)),
            dma((R, N_DP)),
            dma((N_FSDP,)),
            dma((N_FSDP,)),
            dma((2, PIECES, N_DP)),
            dma((N_FSDP, PIECES)),
            dma((N_FSDP, PIECES)),
            dma((N_FSDP, PIECES)),
        ],
        compiler_params=pltpu.CompilerParams(
            collective_id=0, has_side_effects=True, vmem_limit_bytes=40 * 1024 * 1024
        ),
        cost_estimate=pl.CostEstimate(flops=16 * 10**9, bytes_accessed=24 * 10**6, transcendentals=0),
        name="shampoo",
    )(
        *[
            pltpu.with_memory_space_constraint(array, pltpu.HBM)
            for array in (
                grads.reshape(HOMEB, NZ, 2, R, RR, BS), owner, roster,
                left_stats[0, 0], right_stats[0, 0], left_root[0, 0], right_root[0, 0],
            )
        ],
    )
    result, new_left, new_right, roots_left, roots_right = pl.pallas_call(
        finish,
        out_shape=(
            shape((HOMEB, ROWS, BS), BF),
            shape((2, BS, BS), F32),
            shape((2, BS, BS), F32),
            shape((2, BS, BS), BF),
            shape((2, BS, BS), BF),
        ),
        in_specs=[anywhere] * 3,
        out_specs=[anywhere] * 5,
        scratch_shapes=[dma((9,))],
        compiler_params=pltpu.CompilerParams(vmem_limit_bytes=2 * 1024 * 1024),
        name="finish",
    )(*[pltpu.with_memory_space_constraint(out, pltpu.VMEM) for out in outs])
    return (result, new_left[None, None], new_right[None, None], roots_left[None, None], roots_right[None, None])


def solution(mesh):
    placed = P("dp", "fsdp", None, None, None)
    return jax.shard_map(
        local,
        mesh=mesh,
        in_specs=(P("dp", "fsdp", None, None), P(), P(), placed, placed, placed, placed),
        out_specs=(P("fsdp", "dp", None), placed, placed, placed, placed),
        check_vma=False,
    )
```

time: 100 us -> 87.3 us (0.87)
  the two profiles are of different devices: /device:TPU:15 before, /device:TPU:9 now
where the time goes in v1:
time: 87.3 us; the launch traced here: 87.2 us
  Pallas kernels  86.5 us (99%)
    pallas_call x1, Pallas kernels, local(): pl.pallas_call(kernel, out_shape=(pltpu.VMEM((HOMEB, ROWS, BS), BF), pltp...  83.5 us
    pallas_call x1, Pallas kernels, local(): pl.pallas_call(finish, out_shape=(shape((HOMEB, ROWS, BS), BF), shape((2,...  3.03 us

profile of v1, /device:TPU:9, one launch (start us, length us, event | category | flops | bytes accessed | tf_op | source)
XLA Modules:
  0.0 87.2 jit_solution(10553441531846110525)
XLA Ops:
  0.6 83.5 %shampoo.1 = (bf16[14,64,512]{2,1,0:T(8,128)(2,1)S(1)}, f32[2,2,512,512]{3,2,1,0:T(8,128)S(1)}, bf16[2,2,512,512]{3,2,1,0:T(8,128)(2,1)S(1)}) custom-call(bf16[14,4,2,4,16,512]{5,4,3,2,1,0:T(8,128)(2,1)} %bitcast.9, s32[224]{0:T(256)} %owner_in.1, s32[224]{0:T(256)} %roster_in.1, f32[2,512,512]{2,1,0:T(8,128)} %bitcast.10, f32[2,512,512]{2,1,0:T(8,128)} %bitcast.11, ...), custom_call_target="tpu_custom_call" | custom-call | flops 16000000000 | bytes 24000000 | tf_op jit(solution)/shard_map/shampoo/pallas_call | solution.py:524
  84.1 3.0 %finish.1 = (bf16[14,64,512]{2,1,0:T(8,128)(2,1)}, f32[2,512,512]{2,1,0:T(8,128)}, f32[2,512,512]{2,1,0:T(8,128)}, bf16[2,512,512]{2,1,0:T(8,128)(2,1)}, bf16[2,512,512]{2,1,0:T(8,128)(2,1)}) custom-call(bf16[14,64,512]{2,1,0:T(8,128)(2,1)S(1)} %get-tuple-element.13.res, f32[2,2,512,512]{3,2,1,0:T(8,128)S(1)} %get-tuple-element.14.st, ...), custom_call_target="tpu_custom_call" | custom-call | tf_op jit(solution)/shard_map/finish/pallas_call | solution.py:587

commit v2 on v1

--- a/solution.py
+++ b/solution.py
@@ -34,11 +34,10 @@
 
 def kernel(
     grads, owner_in, roster_in, left_stats, right_stats, left_root, right_root,
-    res, st, keep,
+    back, st, keep,
     own, peer, mix, b1p, b1m, b2p, b2m, fin, snd, rcv, grad,
-    mat, fac, cur, upd, turn, back, idx, owner, roster,
-    own_sem, in_sem, core_s, core_r, x_s, x_r, z_s, z_r, pl_s, pl_r, dp_s, dp_r, ex_s, ex_r,
-    h1_s, h1_r, h2_s, h2_r,
+    mat, fac, cur, upd, turn, idx, owner, roster,
+    own_sem, in_sem, sent, first_r, core_r, x_r, z_r, pl_r, dp_r, ex_r, h1_r, h2_r,
 ):
     d = lax.axis_index("dp")
     h = lax.axis_index("fsdp")
@@ -65,7 +64,13 @@
         )
 
     def core_copy(r):
-        return remote(grads.at[:, :, 1 - core, r], peer.at[r], core_s.at[r], core_r.at[r], at_dp(2 * z + 1 - core))
+        return remote(grads.at[:, :, 1 - core, r], peer.at[r], sent.at[0], core_r.at[r], at_dp(2 * z + 1 - core))
+
+    def first_copy(i):
+        q = (far, up, down, z)[i]
+        return remote(
+            grads.at[:, q, 1 - core, 0], peer.at[0, :, q], sent.at[0], first_r.at[i], at_dp(2 * z + 1 - core)
+        )
 
     dev_up = at_dp(2 * up + core)
     dev_down = at_dp(2 * down + core)
@@ -89,48 +94,33 @@
             src, dst, dev = part.at[lo, up], b2p.at[r, lo], dev_up
         else:
             src, dst, dev = part.at[hi, down], b2m.at[r, hi], dev_down
-        return remote(src, dst, z_s.at[kind, r], z_r.at[kind, r], dev)
+        return remote(src, dst, sent.at[1], z_r.at[min(kind, 2), r], dev)
 
     def x_send(i):
         q = (x + i) % 4
-        return remote(own.at[LAST, :, q], mix.at[:, x], x_s.at[q], x_r.at[x], at_fsdp(4 * q + y))
-
-    def x_recv(i):
-        q = (x + i) % 4
-        return remote(own.at[LAST, :, q], mix.at[:, q], x_s.at[q], x_r.at[q], at_fsdp(4 * q + y))
+        return remote(own.at[LAST, :, q], mix.at[:, x], sent.at[2], x_r, at_fsdp(4 * q + y))
+
+    def arrived(ref, semaphore):
+        remote(ref, ref, sent.at[0], semaphore, dev_up).wait_recv()
+
+    def left(ref, kind):
+        remote(ref, ref, sent.at[kind], x_r, dev_up).wait_send()
 
     def plane_send(r, o):
-        return remote(snd.at[r, o], rcv.at[r, h], pl_s.at[r, o], pl_r.at[r, h], at_fsdp(o))
-
-    def plane_recv(r, o):
-        return remote(snd.at[r, o], rcv.at[r, o], pl_s.at[r, o], pl_r.at[r, o], at_fsdp(o))
+        return remote(snd.at[r, o], rcv.at[r, h], sent.at[3], pl_r.at[r], at_fsdp(o))
 
     def rows_of(x, r):
         return pl.ds(pl.multiple_of(x * ROWS + r * RR, RR), RR)
 
     def dp_send(r, x):
-        return remote(
-            rcv.at[r, pl.ds(2 * x, 2)], grad.at[:, rows_of(d, r)], dp_s.at[r, x], dp_r.at[r, d], at_dp(x)
-        )
-
-    def dp_recv(r, x):
-        return remote(
-            rcv.at[r, pl.ds(2 * x, 2)], grad.at[:, rows_of(x, r)], dp_s.at[r, x], dp_r.at[r, x], at_dp(x)
-        )
+        return remote(rcv.at[r, pl.ds(2 * x, 2)], grad.at[:, rows_of(d, r)], sent.at[4], dp_r, at_dp(x))
 
     def ex_send(o):
         return remote(
-            snd.at[LAST, o], grad.at[y % 2, rows_of(2 * x + core, LAST)],
-            ex_s.at[o], ex_r.at[(y % 2) * N_DP + 2 * x + core],
+            snd.at[LAST, o], grad.at[y % 2, rows_of(2 * x + core, LAST)], sent.at[5], ex_r,
             {"dp": 2 * z + y // 2, "fsdp": o},
         )
 
-    def ex_recv(i):
-        return remote(
-            snd.at[LAST, 0], grad.at[i // N_DP, rows_of(i % N_DP, LAST)], ex_s.at[0], ex_r.at[i],
-            {"dp": d, "fsdp": (h + 1) % N_FSDP},
-        )
-
     def chunk(x):
         return pl.ds(pl.multiple_of(x * ROWS, ROWS), ROWS)
 
@@ -138,18 +128,10 @@
         return pl.ds(pl.multiple_of(x * ROWS + p * PIECE, PIECE), PIECE)
 
     def h1_send(j, p, x):
-        return remote(
-            upd.at[j, piece(x, p)], turn.at[2 * d + j, p], h1_s.at[j, p, x], h1_r.at[2 * d + j, p], at_dp(x)
-        )
-
-    def h1_recv(g, p, x):
-        return remote(upd.at[0, piece(x, p)], turn.at[g, p], h1_s.at[0, p, x], h1_r.at[g, p], at_dp(x))
+        return remote(upd.at[j, piece(x, p)], turn.at[2 * d + j, p], sent.at[6], h1_r.at[2 * d + j, p], at_dp(x))
 
     def h2_send(g, p):
-        return remote(turn.at[g, p], back.at[h, p], h2_s.at[g, p], h2_r.at[h, p], at_fsdp(g))
-
-    def h2_recv(o, p):
-        return remote(turn.at[o, p], back.at[o, p], h2_s.at[o, p], h2_r.at[o, p], at_fsdp(o))
+        return remote(turn.at[g, p], back.at[h, p], sent.at[7], h2_r, at_fsdp(g))
 
     def stat_in(i):
         return pltpu.make_async_copy((left_stats, right_stats)[i], st.at[i], in_sem.at[i])
@@ -170,42 +152,43 @@
 
     barrier = pltpu.get_barrier_semaphore()
 
-    @pl.loop(1, N_DP)
-    def _(i):
-        pl.semaphore_signal(barrier, inc=1, device_id=at_dp((d + i) % N_DP), device_id_type=MESH)
-
-    @pl.loop(1, N_FSDP)
-    def _(i):
-        pl.semaphore_signal(barrier, inc=1, device_id=at_fsdp((h + i) % N_FSDP), device_id_type=MESH)
-
     @pl.loop(0, N_DP)
     def _(i):
         there = {"dp": 2 * z + 1 - core, "fsdp": (i // 2) * 4 + 2 * core + i % 2}
         pl.semaphore_signal(barrier, inc=1, device_id=there, device_id_type=MESH)
 
+    @pl.loop(1, N_FSDP)
+    def _(i):
+        pl.semaphore_signal(barrier, inc=1, device_id=at_fsdp((h + 5 * i) % N_FSDP), device_id_type=MESH)
+
+    @pl.loop(1, N_DP)
+    def _(i):
+        pl.semaphore_signal(barrier, inc=1, device_id=at_dp((d + 3 * i) % N_DP), device_id_type=MESH)
+
+    for i in range(2):
+        stat_in(i).start()
+    for i in range(2):
+        keep_in(i).start()
+    for table in tables:
+        table.wait()
+
+    @pl.loop(0, N_FSDP)
+    def _(o):
+        for i, home in enumerate((h, 4 * z + y)):
+            place = jnp.int32(HOMEB)
+            for k in range(HOMEB):
+                place = jnp.where(owner[home * HOMEB + k] == o, jnp.int32(k), place)
+            idx[i, o] = place
+
+    fin[HOMEB] = jnp.zeros((RR, BS), BF)
+
     pl.semaphore_wait(barrier, N_DP + N_FSDP - 2 + jnp.where(y // 2 == core, 0, N_FSDP))
 
-    core_copy(0).start()
+    for i in range(NZ):
+        first_copy(i).start()
     core_copy(LAST).start()
 
     def begin():
-        for i in range(2):
-            stat_in(i).start()
-        for i in range(2):
-            keep_in(i).start()
-
-        for table in tables:
-            table.wait()
-
-        @pl.loop(0, N_FSDP)
-        def _(o):
-            for i, home in enumerate((h, 4 * z + y)):
-                place = jnp.int32(HOMEB)
-                for k in range(HOMEB):
-                    place = jnp.where(owner[home * HOMEB + k] == o, jnp.int32(k), place)
-                idx[i, o] = place
-
-        fin[HOMEB] = jnp.zeros((RR, BS), BF)
         for i in range(2):
             stat_in(i).wait()
         for i in range(2):
@@ -256,10 +239,6 @@
         own_copy(r).wait()
         core_copy(r).wait_recv()
 
-        @pl.when(r == 0)
-        def _():
-            core_copy(1).start()
-
         @pl.when(r == LAST)
         def _():
             core_copy(2).start()
@@ -267,6 +246,15 @@
         @pl.loop(0, HOMEB)
         def _(k):
             own[r, k] = own[r, k] + peer[r, k]
+
+    def stage_a0():
+        own_copy(0).wait()
+        for i, q in enumerate((far, up, down, z)):
+            first_copy(i).wait_recv()
+            own[0, :, q] = own[0, :, q] + peer[0, :, q]
+            for kind in ((0, 1), (2,), (3,), ())[i]:
+                z_copy(kind, 0, False).start()
+        core_copy(1).start()
 
     def begin_z(r, mixed):
         for kind in range(2):
@@ -283,8 +271,7 @@
         mix[:, x] = own[LAST, :, x]
 
     def end_x():
-        for i in (2, 1, 3):
-            x_recv(i).wait_recv()
+        arrived(mix.at[:, pl.ds(0, 3)], x_r)
         begin_z(LAST, True)
 
     def stage_b(r, mixed):
@@ -303,8 +290,7 @@
 
     def stage_c(r, mixed):
         part = held(r, mixed)
-        for kind in range(2, 6):
-            z_copy(kind, r, mixed).wait_recv()
+        arrived(peer.at[r, lo], z_r.at[2, r])
 
         fin[pl.ds(0, HOMEB)] = (
             part[:, z].astype(F32) + b2p[r].astype(F32) + b2m[r].astype(F32)
@@ -334,28 +320,30 @@
                 plane_send(r, (h + 5 * i) % N_FSDP).start()
 
     def stage_d(r):
-        @pl.loop(1, N_FSDP)
-        def _(i):
-            plane_recv(r, (h + i) % N_FSDP).wait_recv()
-
+        arrived(rcv.at[r, pl.ds(0, N_FSDP - 1)], pl_r.at[r])
         grad[:, rows_of(d, r)] = rcv[r, pl.ds(2 * d, 2)]
 
         @pl.loop(1, N_DP)
         def _(i):
             dp_send(r, (d + 3 * i) % N_DP).start()
 
+    def roots_before(t):
+        return jnp.clip(jnp.minimum(2 * (t - 2), t), 0, ROOT_STEPS)
+
     def either(t, *steps):
         return functools.reduce(jnp.logical_or, [t == step for step in steps])
 
-    @pl.loop(0, STEPS)
+    stage_a0()
+
+    @pl.loop(1, STEPS)
     def _(t):
         @pl.when(t < R)
         def _():
-            stage_a(jnp.where(t == 1, LAST, jnp.maximum(t - 1, 0)))
-
-        @pl.when(either(t, 0, 2, 3))
-        def _():
-            begin_z(jnp.maximum(t - 1, 0), False)
+            stage_a(jnp.where(t == 1, LAST, t - 1))
+
+        @pl.when(either(t, 2, 3))
+        def _():
+            begin_z(t - 1, False)
 
         @pl.when(t == 1)
         def _():
@@ -389,24 +377,19 @@
         def _():
             stage_c(LAST, True)
 
-        @pl.when(jnp.logical_and(t >= 2, t < 2 + ROOT_STEPS))
-        def _():
-            root_step(t - 2)
-
-    def from_me(i):
-        return jnp.logical_and(i == (y % 2) * N_DP + 2 * x + core, y // 2 == core)
-
-    @pl.loop(0, LAST)
-    def _(r):
-        @pl.loop(1, N_DP)
-        def _(i):
-            dp_recv(r, (d + i) % N_DP).wait_recv()
-
-    @pl.loop(0, 2 * N_DP)
-    def _(i):
-        @pl.when(jnp.logical_not(from_me(i)))
-        def _():
-            ex_recv(i).wait_recv()
+        @pl.loop(roots_before(t), roots_before(t + 1))
+        def _(step):
+            root_step(step)
+
+    arrived(rcv.at[pl.ds(0, LAST), pl.ds(0, 2 * N_DP - 2)], dp_r)
+
+    @pl.when(y // 2 == core)
+    def _():
+        arrived(snd.at[LAST, pl.ds(0, N_FSDP - 1)], ex_r)
+
+    @pl.when(y // 2 != core)
+    def _():
+        arrived(snd.at[LAST], ex_r)
 
     @pl.loop(0, 2)
     def _(j):
@@ -432,7 +415,7 @@
 
         @pl.when(i > 0)
         def _():
-            h1_recv(g, p, x).wait_recv()
+            arrived(turn.at[g, p], h1_r.at[g, p])
 
         @pl.when(g != h)
         def _():
@@ -456,63 +439,41 @@
         st[0, j] = decay_rate * st[0, j] + (1.0 - decay_rate) * dot(g, g, 1, 1)
         st[1, j] = decay_rate * st[1, j] + (1.0 - decay_rate) * dot(g, g, 0, 0)
 
-    @pl.loop(1, N_FSDP)
-    def _(i):
-        for p in range(PIECES):
-            h2_recv((h + i) % N_FSDP, p).wait_recv()
-
-    @pl.loop(0, HOMEB)
-    def _(k):
-        for p in range(PIECES):
-            res[k, pl.ds(p * PIECE, PIECE)] = back[owner[h * HOMEB + k], p]
-
-    @pl.loop(0, R)
-    def _(r):
-        core_copy(r).wait_send()
-        for kind in range(6):
-            z_copy(kind, r, False).wait_send()
-
-    for i in (1, 2, 3):
-        x_send(i).wait_send()
-
-    @pl.loop(0, LAST)
-    def _(r):
-        @pl.loop(1, N_FSDP)
-        def _(i):
-            plane_send(r, (h + i) % N_FSDP).wait_send()
-
-        @pl.loop(1, N_DP)
-        def _(i):
-            dp_send(r, (d + i) % N_DP).wait_send()
-
-    @pl.loop(1, N_FSDP)
-    def _(i):
-        ex_send((h + i) % N_FSDP).wait_send()
+    arrived(turn.at[pl.ds(0, N_FSDP - 1)], h2_r)
+
+    left(own, 0)
+    left(own.at[pl.ds(0, R - 1)], 1)
+    left(mix.at[:, pl.ds(0, 3)], 2)
+    left(snd.at[pl.ds(0, LAST), pl.ds(0, N_FSDP - 1)], 3)
+    left(rcv.at[pl.ds(0, LAST), pl.ds(0, 2 * N_DP - 2)], 4)
+
+    @pl.when(y // 2 == core)
+    def _():
+        left(snd.at[LAST, pl.ds(0, N_FSDP - 1)], 5)
 
     @pl.when(y // 2 != core)
     def _():
-        ex_send(h).wait_send()
-
-    @pl.loop(0, PIECES)
-    def _(p):
-        @pl.loop(1, N_DP)
-        def _(i):
-            for j in range(2):
-                h1_send(j, p, (d + i) % N_DP).wait_send()
-
-        @pl.loop(1, N_FSDP)
-        def _(i):
-            h2_send((h + i) % N_FSDP, p).wait_send()
-
-
-def finish(res, st, keep, updates, out_sl, out_sr, out_rl, out_rr, sem):
-    copies = [pltpu.make_async_copy(res, updates, sem.at[8])]
+        left(snd.at[LAST], 5)
+
+    left(upd.at[:, pl.ds(0, BS - ROWS)], 6)
+    left(turn.at[pl.ds(0, N_FSDP - 1)], 7)
+
+
+def finish(owner_in, back, st, keep, updates, out_sl, out_sr, out_rl, out_rr, owner, sem):
+    h = lax.axis_index("fsdp")
+    table = pltpu.make_async_copy(owner_in, owner, sem.at[8])
+    table.start()
+    copies = []
     for i in range(2):
         for j in range(2):
             copies.append(pltpu.make_async_copy(st.at[i, j], (out_sl, out_sr)[i].at[j], sem.at[2 * i + j]))
             copies.append(pltpu.make_async_copy(keep.at[i, j], (out_rl, out_rr)[i].at[j], sem.at[4 + 2 * i + j]))
     for copy in copies:
         copy.start()
+    table.wait()
+    for k in range(HOMEB):
+        copies.append(pltpu.make_async_copy(back.at[owner[h * HOMEB + k]], updates.at[k], sem.at[9 + k]))
+        copies[-1].start()
     for copy in copies:
         copy.wait()
 
@@ -524,7 +485,7 @@
     outs = pl.pallas_call(
         kernel,
         out_shape=(
-            pltpu.VMEM((HOMEB, ROWS, BS), BF),
+            pltpu.VMEM((N_FSDP, PIECES, PIECE, BS), BF),
             pltpu.VMEM((2, 2, BS, BS), F32),
             pltpu.VMEM((2, 2, BS, BS), BF),
         ),
@@ -547,28 +508,21 @@
             pltpu.VMEM((2, BS, BS), BF),
             pltpu.VMEM((2, BS, BS), BF),
             pltpu.VMEM((N_FSDP, PIECES, PIECE, BS), BF),
-            pltpu.VMEM((N_FSDP, PIECES, PIECE, BS), BF),
             pltpu.SMEM((2, N_FSDP), jnp.int32),
             pltpu.SMEM((N_FSDP * HOMEB,), jnp.int32),
             pltpu.SMEM((N_FSDP * HOMEB,), jnp.int32),
             dma((R,)),
             dma((6,)),
+            dma((8,)),
+            dma((NZ,)),
             dma((R,)),
-            dma((R,)),
-            dma((4,)),
-            dma((4,)),
-            dma((6, R)),
-            dma((6, R)),
-            dma((R, N_FSDP)),
-            dma((R, N_FSDP)),
-            dma((R, N_DP)),
-            dma((R, N_DP)),
-            dma((N_FSDP,)),
-            dma((N_FSDP,)),
-            dma((2, PIECES, N_DP)),
+            dma,
+            dma((3, R)),
+            dma((LAST,)),
+            dma,
+            dma,
             dma((N_FSDP, PIECES)),
-            dma((N_FSDP, PIECES)),
-            dma((N_FSDP, PIECES)),
+            dma,
         ],
         compiler_params=pltpu.CompilerParams(
             collective_id=0, has_side_effects=True, vmem_limit_bytes=40 * 1024 * 1024
@@ -587,18 +541,22 @@
     result, new_left, new_right, roots_left, roots_right = pl.pallas_call(
         finish,
         out_shape=(
-            shape((HOMEB, ROWS, BS), BF),
+            shape((HOMEB, PIECES, PIECE, BS), BF),
             shape((2, BS, BS), F32),
             shape((2, BS, BS), F32),
             shape((2, BS, BS), BF),
             shape((2, BS, BS), BF),
         ),
-        in_specs=[anywhere] * 3,
+        in_specs=[anywhere] * 4,
         out_specs=[anywhere] * 5,
-        scratch_shapes=[dma((9,))],
+        scratch_shapes=[pltpu.SMEM((N_FSDP * HOMEB,), jnp.int32), dma((9 + HOMEB,))],
         compiler_params=pltpu.CompilerParams(vmem_limit_bytes=2 * 1024 * 1024),
         name="finish",
-    )(*[pltpu.with_memory_space_constraint(out, pltpu.VMEM) for out in outs])
+    )(
+        pltpu.with_memory_space_constraint(owner, pltpu.HBM),
+        *[pltpu.with_memory_space_constraint(out, pltpu.VMEM) for out in outs],
+    )
+    result = result.reshape(HOMEB, ROWS, BS)
     return (result, new_left[None, None], new_right[None, None], roots_left[None, None], roots_right[None, None])
 
 

time: 87.3 us -> 80.6 us (0.923)
  the two profiles are of different devices: /device:TPU:9 before, /device:TPU:1 now
where the time goes in v2:
time: 80.6 us; the launch traced here: 80.2 us
  Pallas kernels  79.5 us (99%)
    pallas_call x1, Pallas kernels, local(): pl.pallas_call(kernel, out_shape=(pltpu.VMEM((N_FSDP, PIECES, PIECE, BS),...  76.4 us
    pallas_call x1, Pallas kernels, local(): pl.pallas_call(finish, out_shape=(shape((HOMEB, PIECES, PIECE, BS), BF),...  3.1 us

profile of v2, /device:TPU:1, one launch (start us, length us, event | category | flops | bytes accessed | tf_op | source)
XLA Modules:
  0.0 80.2 jit_solution(14885437105753492200)
XLA Ops:
  0.6 76.4 %shampoo.1 = (bf16[16,2,32,512]{3,2,1,0:T(8,128)(2,1)S(1)}, f32[2,2,512,512]{3,2,1,0:T(8,128)S(1)}, bf16[2,2,512,512]{3,2,1,0:T(8,128)(2,1)S(1)}) custom-call(bf16[14,4,2,4,16,512]{5,4,3,2,1,0:T(8,128)(2,1)} %bitcast.10, s32[224]{0:T(256)} %owner_in.3, s32[224]{0:T(256)} %roster_in.1, f32[2,512,512]{2,1,0:T(8,128)} %bitcast.11, f32[2,512,512]{2,1,0:T(8,128)} %bitcast.12, ...), custom_call_target="tpu_custom_call" | custom-call | flops 16000000000 | bytes 24000000 | tf_op jit(solution)/shard_map/shampoo/pallas_call | solution.py:485
  77.1 3.1 %finish.1 = (bf16[14,2,32,512]{3,2,1,0:T(8,128)(2,1)}, f32[2,512,512]{2,1,0:T(8,128)}, f32[2,512,512]{2,1,0:T(8,128)}, bf16[2,512,512]{2,1,0:T(8,128)(2,1)}, bf16[2,512,512]{2,1,0:T(8,128)(2,1)}) custom-call(s32[224]{0:T(256)} %owner_in.3, bf16[16,2,32,512]{3,2,1,0:T(8,128)(2,1)S(1)} %get-tuple-element.13.back, f32[2,2,512,512]{3,2,1,0:T(8,128)S(1)} %get-tuple-element.14.st, ...), custom_call_target="tpu_custom_call" | custom-call | tf_op jit(solution)/shard_map/finish/pallas_call | solution.py:541

commit v3 on v2

--- a/solution.py
+++ b/solution.py
@@ -19,7 +19,7 @@
 LAST = R - 1
 ROOT_STEPS = 6
 STEPS = 9
-PIECES = 2
+PIECES = 4
 PIECE = ROWS // PIECES
 decay_rate = 0.9
 learn_rate = 10.0
@@ -357,17 +357,17 @@
         def _():
             stage_b(t - 2, False)
 
+        @pl.when(either(t, 4, 5, 6))
+        def _():
+            stage_c(t - 4, False)
+
+        @pl.when(t == 4)
+        def _():
+            end_x()
+
         @pl.when(t == 5)
         def _():
-            end_x()
-
-        @pl.when(t == 6)
-        def _():
             stage_b(LAST, True)
-
-        @pl.when(either(t, 4, 5, 6))
-        def _():
-            stage_c(t - 4, False)
 
         @pl.when(either(t, 5, 6, 7))
         def _():
@@ -405,8 +405,11 @@
         for p in range(PIECES):
             turn[2 * d + j, p] = upd[j, piece(d, p)]
 
-            @pl.loop(1, N_DP)
-            def _(i):
+    @pl.loop(0, PIECES)
+    def _(p):
+        @pl.loop(1, N_DP)
+        def _(i):
+            for j in range(2):
                 h1_send(j, p, (d + 3 * i) % N_DP).start()
 
     def forward(i, j, p):
@@ -425,12 +428,11 @@
         def _():
             back[h, p] = turn[h, p]
 
-    @pl.loop(0, 2)
-    def _(j):
-        @pl.loop(0, PIECES)
-        def _(p):
-            @pl.loop(0, N_DP)
-            def _(i):
+    @pl.loop(0, PIECES)
+    def _(p):
+        @pl.loop(0, N_DP)
+        def _(i):
+            for j in range(2):
                 forward(i, j, p)
 
     @pl.loop(0, 2)

time: 80.6 us -> 77.7 us (0.964)
  Pallas kernels: 79.5 us -> 76.9 us
    pallas_call x1, Pallas kernels: 76.4 us -> 73.8 us  [local(): pl.pallas_call(kernel, out_shape=(pltpu.VMEM((N_FSDP, PIECES, PIECE, BS),...]
where the time goes in v3:
time: 77.7 us; the launch traced here: 77.6 us
  Pallas kernels  76.9 us (99%)
    pallas_call x1, Pallas kernels, local(): pl.pallas_call(kernel, out_shape=(pltpu.VMEM((N_FSDP, PIECES, PIECE, BS),...  73.8 us
    pallas_call x1, Pallas kernels, local(): pl.pallas_call(finish, out_shape=(shape((HOMEB, PIECES, PIECE, BS), BF),...  3.1 us

profile of v3, /device:TPU:1, one launch (start us, length us, event | category | flops | bytes accessed | tf_op | source)
XLA Modules:
  0.0 77.6 jit_solution(7259311004047008608)
XLA Ops:
  0.6 73.8 %shampoo.1 = (bf16[16,4,16,512]{3,2,1,0:T(8,128)(2,1)S(1)}, f32[2,2,512,512]{3,2,1,0:T(8,128)S(1)}, bf16[2,2,512,512]{3,2,1,0:T(8,128)(2,1)S(1)}) custom-call(bf16[14,4,2,4,16,512]{5,4,3,2,1,0:T(8,128)(2,1)} %bitcast.10, s32[224]{0:T(256)} %owner_in.3, s32[224]{0:T(256)} %roster_in.1, f32[2,512,512]{2,1,0:T(8,128)} %bitcast.11, f32[2,512,512]{2,1,0:T(8,128)} %bitcast.12, ...), custom_call_target="tpu_custom_call" | custom-call | flops 16000000000 | bytes 24000000 | tf_op jit(solution)/shard_map/shampoo/pallas_call | solution.py:487
  74.5 3.1 %finish.1 = (bf16[14,4,16,512]{3,2,1,0:T(8,128)(2,1)}, f32[2,512,512]{2,1,0:T(8,128)}, f32[2,512,512]{2,1,0:T(8,128)}, bf16[2,512,512]{2,1,0:T(8,128)(2,1)}, bf16[2,512,512]{2,1,0:T(8,128)(2,1)}) custom-call(s32[224]{0:T(256)} %owner_in.3, bf16[16,4,16,512]{3,2,1,0:T(8,128)(2,1)S(1)} %get-tuple-element.13.back, f32[2,2,512,512]{3,2,1,0:T(8,128)S(1)} %get-tuple-element.14.st, ...), custom_call_target="tpu_custom_call" | custom-call | tf_op jit(solution)/shard_map/finish/pallas_call | solution.py:543

commit v4 on v3

--- a/solution.py
+++ b/solution.py
@@ -260,7 +260,7 @@
         for kind in range(2):
             z_copy(kind, r, mixed).start()
 
-        @pl.when(r != LAST)
+        @pl.when(r < 2)
         def _():
             for kind in range(2, 4):
                 z_copy(kind, r, mixed).start()
@@ -273,6 +273,9 @@
     def end_x():
         arrived(mix.at[:, pl.ds(0, 3)], x_r)
         begin_z(LAST, True)
+        for kind in range(2, 4):
+            z_copy(kind, 2, False).start()
+            z_copy(kind, LAST, True).start()
 
     def stage_b(r, mixed):
         part = held(r, mixed)
@@ -283,11 +286,6 @@
         part[hi, down] = part[hi, down] + b1m[r]
         z_copy(5, r, mixed).start()
 
-        @pl.when(r == LAST)
-        def _():
-            for kind in range(2, 4):
-                z_copy(kind, r, mixed).start()
-
     def stage_c(r, mixed):
         part = held(r, mixed)
         arrived(peer.at[r, lo], z_r.at[2, r])
@@ -328,7 +326,7 @@
             dp_send(r, (d + 3 * i) % N_DP).start()
 
     def roots_before(t):
-        return jnp.clip(jnp.minimum(2 * (t - 2), t), 0, ROOT_STEPS)
+        return jnp.clip(jnp.where(t < 4, 2 * (t - 2), 2 * t - 5), 0, ROOT_STEPS)
 
     def either(t, *steps):
         return functools.reduce(jnp.logical_or, [t == step for step in steps])

time: 77.7 us -> 75.8 us (0.976)
  Pallas kernels: 76.9 us -> 75 us
    pallas_call x1, Pallas kernels: 73.8 us -> 71.9 us  [local(): pl.pallas_call(kernel, out_shape=(pltpu.VMEM((N_FSDP, PIECES, PIECE, BS),...]
where the time goes in v4:
time: 75.8 us; the launch traced here: 75.7 us
  Pallas kernels  75 us (99%)
    pallas_call x1, Pallas kernels, local(): pl.pallas_call(kernel, out_shape=(pltpu.VMEM((N_FSDP, PIECES, PIECE, BS),...  71.9 us
    pallas_call x1, Pallas kernels, local(): pl.pallas_call(finish, out_shape=(shape((HOMEB, PIECES, PIECE, BS), BF),...  3.1 us

profile of v4, /device:TPU:1, one launch (start us, length us, event | category | flops | bytes accessed | tf_op | source)
XLA Modules:
  0.0 75.7 jit_solution(4207693039277445287)
XLA Ops:
  0.6 71.9 %shampoo.1 = (bf16[16,4,16,512]{3,2,1,0:T(8,128)(2,1)S(1)}, f32[2,2,512,512]{3,2,1,0:T(8,128)S(1)}, bf16[2,2,512,512]{3,2,1,0:T(8,128)(2,1)S(1)}) custom-call(bf16[14,4,2,4,16,512]{5,4,3,2,1,0:T(8,128)(2,1)} %bitcast.10, s32[224]{0:T(256)} %owner_in.3, s32[224]{0:T(256)} %roster_in.1, f32[2,512,512]{2,1,0:T(8,128)} %bitcast.11, f32[2,512,512]{2,1,0:T(8,128)} %bitcast.12, ...), custom_call_target="tpu_custom_call" | custom-call | flops 16000000000 | bytes 24000000 | tf_op jit(solution)/shard_map/shampoo/pallas_call | solution.py:485
  72.6 3.1 %finish.1 = (bf16[14,4,16,512]{3,2,1,0:T(8,128)(2,1)}, f32[2,512,512]{2,1,0:T(8,128)}, f32[2,512,512]{2,1,0:T(8,128)}, bf16[2,512,512]{2,1,0:T(8,128)(2,1)}, bf16[2,512,512]{2,1,0:T(8,128)(2,1)}) custom-call(s32[224]{0:T(256)} %owner_in.3, bf16[16,4,16,512]{3,2,1,0:T(8,128)(2,1)S(1)} %get-tuple-element.13.back, f32[2,2,512,512]{3,2,1,0:T(8,128)S(1)} %get-tuple-element.14.st, ...), custom_call_target="tpu_custom_call" | custom-call | tf_op jit(solution)/shard_map/finish/pallas_call | solution.py:541

commit v5 on v4

--- a/solution.py
+++ b/solution.py
@@ -18,7 +18,7 @@
 RR = ROWS // R
 LAST = R - 1
 ROOT_STEPS = 6
-STEPS = 9
+STEPS = 8
 PIECES = 4
 PIECE = ROWS // PIECES
 decay_rate = 0.9
@@ -326,7 +326,7 @@
             dp_send(r, (d + 3 * i) % N_DP).start()
 
     def roots_before(t):
-        return jnp.clip(jnp.where(t < 4, 2 * (t - 2), 2 * t - 5), 0, ROOT_STEPS)
+        return jnp.where(t < 3, 0, jnp.where(t == 3, 1, jnp.where(t == 4, 3, jnp.where(t == 5, 5, ROOT_STEPS))))
 
     def either(t, *steps):
         return functools.reduce(jnp.logical_or, [t == step for step in steps])
@@ -367,13 +367,13 @@
         def _():
             stage_b(LAST, True)
 
+        @pl.when(t == 7)
+        def _():
+            stage_c(LAST, True)
+
         @pl.when(either(t, 5, 6, 7))
         def _():
             stage_d(t - 5)
-
-        @pl.when(t == 8)
-        def _():
-            stage_c(LAST, True)
 
         @pl.loop(roots_before(t), roots_before(t + 1))
         def _(step):

time: 75.8 us -> 75.7 us (level)
  no operation moved by 1% of the time
where the time goes in v5:
time: 75.7 us; the launch traced here: 75.5 us
  Pallas kernels  74.9 us (99%)
    pallas_call x1, Pallas kernels, local(): pl.pallas_call(kernel, out_shape=(pltpu.VMEM((N_FSDP, PIECES, PIECE, BS),...  71.8 us
    pallas_call x1, Pallas kernels, local(): pl.pallas_call(finish, out_shape=(shape((HOMEB, PIECES, PIECE, BS), BF),...  3.1 us

profile of v5, /device:TPU:1, one launch (start us, length us, event | category | flops | bytes accessed | tf_op | source)
XLA Modules:
  0.0 75.5 jit_solution(3469436386648552791)
XLA Ops:
  0.6 71.8 %shampoo.1 = (bf16[16,4,16,512]{3,2,1,0:T(8,128)(2,1)S(1)}, f32[2,2,512,512]{3,2,1,0:T(8,128)S(1)}, bf16[2,2,512,512]{3,2,1,0:T(8,128)(2,1)S(1)}) custom-call(bf16[14,4,2,4,16,512]{5,4,3,2,1,0:T(8,128)(2,1)} %bitcast.10, s32[224]{0:T(256)} %owner_in.3, s32[224]{0:T(256)} %roster_in.1, f32[2,512,512]{2,1,0:T(8,128)} %bitcast.11, f32[2,512,512]{2,1,0:T(8,128)} %bitcast.12, ...), custom_call_target="tpu_custom_call" | custom-call | flops 16000000000 | bytes 24000000 | tf_op jit(solution)/shard_map/shampoo/pallas_call | solution.py:485
  72.4 3.1 %finish.1 = (bf16[14,4,16,512]{3,2,1,0:T(8,128)(2,1)}, f32[2,512,512]{2,1,0:T(8,128)}, f32[2,512,512]{2,1,0:T(8,128)}, bf16[2,512,512]{2,1,0:T(8,128)(2,1)}, bf16[2,512,512]{2,1,0:T(8,128)(2,1)}) custom-call(s32[224]{0:T(256)} %owner_in.3, bf16[16,4,16,512]{3,2,1,0:T(8,128)(2,1)S(1)} %get-tuple-element.13.back, f32[2,2,512,512]{3,2,1,0:T(8,128)S(1)} %get-tuple-element.14.st, ...), custom_call_target="tpu_custom_call" | custom-call | tf_op jit(solution)/shard_map/finish/pallas_call | solution.py:541

commit v6 on v5

--- a/solution.py
+++ b/solution.py
@@ -127,8 +127,8 @@
     def piece(x, p):
         return pl.ds(pl.multiple_of(x * ROWS + p * PIECE, PIECE), PIECE)
 
-    def h1_send(j, p, x):
-        return remote(upd.at[j, piece(x, p)], turn.at[2 * d + j, p], sent.at[6], h1_r.at[2 * d + j, p], at_dp(x))
+    def h1_send(p, x):
+        return remote(upd.at[:, piece(x, p)], turn.at[pl.ds(2 * d, 2), p], sent.at[6], h1_r.at[d, p], at_dp(x))
 
     def h2_send(g, p):
         return remote(turn.at[g, p], back.at[h, p], sent.at[7], h2_r, at_fsdp(g))
@@ -407,16 +407,10 @@
     def _(p):
         @pl.loop(1, N_DP)
         def _(i):
-            for j in range(2):
-                h1_send(j, p, (d + 3 * i) % N_DP).start()
-
-    def forward(i, j, p):
-        x = (d + 5 * i) % N_DP
+            h1_send(p, (d + 3 * i) % N_DP).start()
+
+    def forward(x, j, p):
         g = 2 * x + j
-
-        @pl.when(i > 0)
-        def _():
-            arrived(turn.at[g, p], h1_r.at[g, p])
 
         @pl.when(g != h)
         def _():
@@ -430,8 +424,14 @@
     def _(p):
         @pl.loop(0, N_DP)
         def _(i):
+            x = (d + 5 * i) % N_DP
+
+            @pl.when(i > 0)
+            def _():
+                arrived(turn.at[pl.ds(2 * x, 2), p], h1_r.at[x, p])
+
             for j in range(2):
-                forward(i, j, p)
+                forward(x, j, p)
 
     @pl.loop(0, 2)
     def _(j):
@@ -521,7 +521,7 @@
             dma((LAST,)),
             dma,
             dma,
-            dma((N_FSDP, PIECES)),
+            dma((N_DP, PIECES)),
             dma,
         ],
         compiler_params=pltpu.CompilerParams(

time: 75.7 us -> 75.4 us (level)
  no operation moved by 1% of the time
where the time goes in v6:
time: 75.4 us; the launch traced here: 75.3 us
  Pallas kernels  74.7 us (99%)
    pallas_call x1, Pallas kernels, local(): pl.pallas_call(kernel, out_shape=(pltpu.VMEM((N_FSDP, PIECES, PIECE, BS),...  71.6 us
    pallas_call x1, Pallas kernels, local(): pl.pallas_call(finish, out_shape=(shape((HOMEB, PIECES, PIECE, BS), BF),...  3.1 us

profile of v6, /device:TPU:1, one launch (start us, length us, event | category | flops | bytes accessed | tf_op | source)
XLA Modules:
  0.0 75.3 jit_solution(13696055401301844917)
XLA Ops:
  0.6 71.6 %shampoo.1 = (bf16[16,4,16,512]{3,2,1,0:T(8,128)(2,1)S(1)}, f32[2,2,512,512]{3,2,1,0:T(8,128)S(1)}, bf16[2,2,512,512]{3,2,1,0:T(8,128)(2,1)S(1)}) custom-call(bf16[14,4,2,4,16,512]{5,4,3,2,1,0:T(8,128)(2,1)} %bitcast.10, s32[224]{0:T(256)} %owner_in.3, s32[224]{0:T(256)} %roster_in.1, f32[2,512,512]{2,1,0:T(8,128)} %bitcast.11, f32[2,512,512]{2,1,0:T(8,128)} %bitcast.12, ...), custom_call_target="tpu_custom_call" | custom-call | flops 16000000000 | bytes 24000000 | tf_op jit(solution)/shard_map/shampoo/pallas_call | solution.py:485
  72.2 3.1 %finish.1 = (bf16[14,4,16,512]{3,2,1,0:T(8,128)(2,1)}, f32[2,512,512]{2,1,0:T(8,128)}, f32[2,512,512]{2,1,0:T(8,128)}, bf16[2,512,512]{2,1,0:T(8,128)(2,1)}, bf16[2,512,512]{2,1,0:T(8,128)(2,1)}) custom-call(s32[224]{0:T(256)} %owner_in.3, bf16[16,4,16,512]{3,2,1,0:T(8,128)(2,1)S(1)} %get-tuple-element.13.back, f32[2,2,512,512]{3,2,1,0:T(8,128)S(1)} %get-tuple-element.14.st, ...), custom_call_target="tpu_custom_call" | custom-call | tf_op jit(solution)/shard_map/finish/pallas_call | solution.py:541
